TPU v7x, 32 devices: a whole 2x2x4 slice. The times are simulated.
32 devices in a mesh: ha: 4 (over y, x), wa: 8 (over z, core).
Axes of the slice: x: 2, y: 2, z: 4, core: 2. Of those that a mesh axis runs over, the one named last changes fastest.
Arguments:
- velocity: float32 [2, 256, 1024], P(None, 'wa', 'ha'), may hold values from -6 to 6
- cotangent: float32 [2, 256, 1024], P(None, 'wa', 'ha'), may hold values from -6 to 6
- lift_weight: float32 [64, 2], replicated, may hold values from -4 to 4
- depth_kernels: float32 [1, 64, 9], replicated, may hold values from -2 to 2
- point_weights: bfloat16 [1, 64, 64], replicated, may hold values from -0.75 to 0.75
- out_weight: bfloat16 [2, 64], replicated, may hold values from -0.75 to 0.75
Outputs:
- grad_velocity: float32 [2, 256, 1024], P(None, 'wa', 'ha')
- grad_lift: float32 [64, 2], replicated
- grad_kernels: float32 [1, 64, 9], replicated
- grad_point: float32 [1, 64, 64], replicated
- grad_out: float32 [2, 64], replicated
All inputs are finite; a program needn't handle non-finite values.
Results may differ from a plain program's by a relative error of at most 0.012.
Values may be sent and summed in bfloat16 or wider, within the bound.
A program may use at most 64 MiB of HBM per device.

v0:
```python
import functools
import math

import jax
import jax.numpy as jnp
import ml_dtypes
import numpy as np
from jax import lax
from jax.experimental import pallas as pl
from jax.experimental.pallas import tpu as pltpu
from jax.sharding import PartitionSpec as P

OFFSETS = ((-1, -1), (-1, 0), (-1, 1), (0, -1), (0, 0), (0, 1), (1, -1), (1, 0), (1, 1))
TWO_PI = 2.0 * math.pi


def extended(value, sides, width):
    for axis, dim in sides:
        size, length = (lax.axis_size(axis), value.shape[dim])
        up = [(i, (i + 1) % size) for i in range(size)]
        down = [(j, i) for i, j in up]
        last = lax.slice_in_dim(value, length - width, length, axis=dim)
        leading = lax.slice_in_dim(value, 0, width, axis=dim)
        before = lax.ppermute(last, axis, up)
        after = lax.ppermute(leading, axis, down)
        value = jnp.concatenate([before, value, after], axis=dim)
    return value


def dft_table(table_len, sign_val):
    ids = jnp.arange(table_len, dtype=jnp.int32)
    product = ids[:, None] * ids[None, :] % table_len
    phase_angle = sign_val * TWO_PI / table_len * product.astype(jnp.float32)
    return (jnp.cos(phase_angle), jnp.sin(phase_angle))


def apply_table(values, tab_real, tab_imag):
    highest = lax.Precision.HIGHEST
    real_part = values[0]
    imag_part = values[1]
    out_real = jnp.einsum("...n,kn->...k", real_part, tab_real, precision=highest) - jnp.einsum(
        "...n,kn->...k", imag_part, tab_imag, precision=highest
    )
    out_imag = jnp.einsum("...n,kn->...k", real_part, tab_imag, precision=highest) + jnp.einsum(
        "...n,kn->...k", imag_part, tab_real, precision=highest
    )
    return jnp.stack([out_real, out_imag])


def rotate(values, phase_angle):
    cosine = jnp.cos(phase_angle)
    sine_val = jnp.sin(phase_angle)
    return jnp.stack(
        [values[0] * cosine - values[1] * sine_val, values[0] * sine_val + values[1] * cosine]
    )


def forward_first(values, axis_dim, groups, own_index, length):
    moved = jnp.moveaxis(values, axis_dim, -1)
    leading = moved.shape[:-1]
    full_len = moved.shape[-1]
    piece_len = full_len // groups
    moved = jnp.swapaxes(moved.reshape(leading + (groups, piece_len)), -1, -2)
    tab_real, tab_imag = dft_table(groups, -1.0)
    moved = apply_table(moved, tab_real, tab_imag)
    local_m = jnp.arange(piece_len, dtype=jnp.int32)[:, None] + own_index * piece_len
    first_k = jnp.arange(groups, dtype=jnp.int32)[None, :]
    phase_angle = -TWO_PI / length * (local_m * first_k % length).astype(jnp.float32)
    moved = rotate(moved, phase_angle)
    moved = jnp.swapaxes(moved, -1, -2).reshape(leading + (full_len,))
    return jnp.moveaxis(moved, -1, axis_dim)


def forward_second(values, axis_dim):
    moved = jnp.moveaxis(values, axis_dim, -1)
    tab_real, tab_imag = dft_table(moved.shape[-1], -1.0)
    moved = apply_table(moved, tab_real, tab_imag)
    return jnp.moveaxis(moved, -1, axis_dim)


def inverse_first(values, axis_dim, own_index, length):
    moved = jnp.moveaxis(values, axis_dim, -1)
    full_len = moved.shape[-1]
    tab_real, tab_imag = dft_table(full_len, 1.0)
    moved = apply_table(moved, tab_real, tab_imag)
    local_m = jnp.arange(full_len, dtype=jnp.int32)
    phase_angle = TWO_PI / length * (local_m * own_index % length).astype(jnp.float32)
    moved = rotate(moved, phase_angle)
    return jnp.moveaxis(moved, -1, axis_dim)


def inverse_second(values, axis_dim, groups):
    moved = jnp.moveaxis(values, axis_dim, -1)
    leading = moved.shape[:-1]
    full_len = moved.shape[-1]
    piece_len = full_len // groups
    moved = jnp.swapaxes(moved.reshape(leading + (groups, piece_len)), -1, -2)
    tab_real, tab_imag = dft_table(groups, 1.0)
    moved = apply_table(moved, tab_real, tab_imag)
    moved = jnp.swapaxes(moved, -1, -2).reshape(leading + (full_len,))
    return jnp.moveaxis(moved, -1, axis_dim)


def signed_waves(own_index, groups, count_n):
    ids = own_index + groups * jnp.arange(count_n, dtype=jnp.int32)
    total_len = groups * count_n
    return jnp.where(2 * ids >= total_len, ids - total_len, ids).astype(jnp.float32)


def project(spectrum, wave_x, wave_y):
    along_k = wave_x * spectrum[:, 0] + wave_y * spectrum[:, 1]
    factor = along_k / jnp.maximum(wave_x * wave_x + wave_y * wave_y, 1.0)
    return jnp.stack([spectrum[:, 0] - wave_x * factor, spectrum[:, 1] - wave_y * factor], axis=1)


def depthwise_valid(padded, kernel):
    rows_in = padded.shape[1] - 2
    cols_in = padded.shape[2] - 2
    total = jnp.zeros((padded.shape[0], rows_in, cols_in), jnp.float32)
    for offset_id in range(9):
        step_x, step_y = OFFSETS[offset_id]
        total = (
            total
            + kernel[:, offset_id][:, None, None]
            * padded[:, 1 + step_x : 1 + step_x + rows_in, 1 + step_y : 1 + step_y + cols_in]
        )
    return total


def transposed_add(grad_hidden, grad_pad, kernel):
    rows_in = grad_hidden.shape[1]
    cols_in = grad_hidden.shape[2]
    for offset_id in range(9):
        step_x, step_y = OFFSETS[offset_id]
        grad_hidden = (
            grad_hidden
            + kernel[:, offset_id][:, None, None]
            * grad_pad[:, 1 - step_x : 1 - step_x + rows_in, 1 - step_y : 1 - step_y + cols_in]
        )
    return grad_hidden


def kernel_grad(grad_depth, padded):
    rows_in = grad_depth.shape[1]
    cols_in = grad_depth.shape[2]
    grad_full = grad_depth.astype(jnp.float32)
    entries = []
    for offset_id in range(9):
        step_x, step_y = OFFSETS[offset_id]
        window = padded[
            :, 1 + step_x : 1 + step_x + rows_in, 1 + step_y : 1 + step_y + cols_in
        ].astype(jnp.float32)
        entries.append(jnp.sum(grad_full * window, axis=(1, 2)))
    return jnp.stack(entries, axis=1)


def local(velocity, cotangent, lift_weight, depth_kernels, point_weights, out_weight):
    highest = lax.Precision.HIGHEST
    layers = depth_kernels.shape[0]
    cols_n = velocity.shape[1]
    rows_n = velocity.shape[2]
    groups_x = lax.axis_size("wa")
    groups_y = lax.axis_size("ha")
    own_x = lax.axis_index("wa")
    own_y = lax.axis_index("ha")
    length_x = cols_n * groups_x
    length_y = rows_n * groups_y
    spectrum = jnp.stack([cotangent, jnp.zeros_like(cotangent)])
    wave_x = signed_waves(own_x, groups_x, cols_n)[:, None]
    wave_y = signed_waves(own_y, groups_y, rows_n)[None, :]

    def move_x(values):
        return lax.all_to_all(values, "wa", split_axis=2, concat_axis=2, tiled=True)

    def move_y(values):
        return lax.all_to_all(values, "ha", split_axis=3, concat_axis=3, tiled=True)

    spectrum = forward_first(move_x(spectrum), 2, groups_x, own_x, length_x)
    spectrum = forward_second(move_x(spectrum), 2)
    spectrum = forward_first(move_y(spectrum), 3, groups_y, own_y, length_y)
    spectrum = forward_second(move_y(spectrum), 3)
    spectrum = project(spectrum, wave_x, wave_y)
    spectrum = move_y(inverse_first(spectrum, 3, own_y, length_y))
    spectrum = move_y(inverse_second(spectrum, 3, groups_y))
    spectrum = move_x(inverse_first(spectrum, 2, own_x, length_x))
    spectrum = move_x(inverse_second(spectrum, 2, groups_x))
    grad_proj = spectrum[0] / float(length_x * length_y)
    saved_pad, saved_depth, saved_tanh = ([], [], [])
    hidden = jnp.einsum("cs,sxy->cxy", lift_weight, velocity, precision=highest).astype(
        jnp.bfloat16
    )
    layer_id = 0
    padded = extended(hidden, (("ha", 2), ("wa", 1)), 1)
    depth_out = depthwise_valid(padded, depth_kernels[layer_id]).astype(jnp.bfloat16)
    mixed_pre = jnp.einsum(
        "oc,cxy->oxy", point_weights[layer_id], depth_out, preferred_element_type=jnp.float32
    )
    squash = jnp.tanh(mixed_pre).astype(jnp.bfloat16)
    saved_pad.append(padded)
    saved_depth.append(depth_out)
    saved_tanh.append(squash)
    hidden = (hidden.astype(jnp.float32) + squash.astype(jnp.float32)).astype(jnp.bfloat16)
    grad_proj_b = grad_proj.astype(jnp.bfloat16)
    out_sum = jnp.einsum("sxy,cxy->sc", grad_proj_b, hidden, preferred_element_type=jnp.float32)
    grad_hidden = jnp.einsum(
        "sc,sxy->cxy", out_weight, grad_proj_b, preferred_element_type=jnp.float32
    )
    kernel_sums = [None] * layers
    point_sums = [None] * layers
    for layer_id in reversed(range(layers)):
        squash_full = saved_tanh[layer_id].astype(jnp.float32)
        grad_mixed = (grad_hidden * (1.0 - squash_full * squash_full)).astype(jnp.bfloat16)
        point_sums[layer_id] = jnp.einsum(
            "oxy,cxy->oc", grad_mixed, saved_depth[layer_id], preferred_element_type=jnp.float32
        )
        grad_depth = jnp.einsum(
            "oc,oxy->cxy", point_weights[layer_id], grad_mixed, preferred_element_type=jnp.float32
        ).astype(jnp.bfloat16)
        grad_pad = extended(grad_depth, (("ha", 2), ("wa", 1)), 1)
        kernel_sums[layer_id] = kernel_grad(grad_depth, saved_pad[layer_id])
        grad_hidden = transposed_add(grad_hidden, grad_pad, depth_kernels[layer_id])
    lift_sum = jnp.einsum("cxy,sxy->cs", grad_hidden, velocity, precision=highest)
    grad_velocity = grad_proj + jnp.einsum(
        "cs,cxy->sxy", lift_weight, grad_hidden, precision=highest
    )
    totals = lax.psum(
        (lift_sum, jnp.stack(kernel_sums), jnp.stack(point_sums), out_sum), ("ha", "wa")
    )
    scale = 1.0 / math.sqrt(length_x * length_y)
    return (
        grad_velocity,
        totals[0] * scale,
        totals[1] * scale,
        totals[2] * scale,
        totals[3] * scale,
    )


def real_basis(pairs, is_sin, positions, length):
    angle = 2.0 * np.pi / length * (np.outer(pairs, positions) % length)
    sines = np.where(pairs[:, None] == 0, np.cos(np.pi * positions)[None, :], np.sin(angle))
    return np.where(is_sin[:, None], sines, np.cos(angle))


def make_tables(groups_y, groups_x, rows, cols):
    length_x, length_y = groups_x * rows, groups_y * cols
    per = length_y // (groups_x * groups_y)
    half = per // 2
    ids = np.arange(length_y)
    pair_y = (ids // per) * half + ids % half
    sin_y = (ids % per) >= half
    forward_y = real_basis(pair_y, sin_y, np.arange(length_y), length_y)
    forward_y = forward_y.reshape(groups_y, cols, length_y)
    lanes = np.arange(cols + 128)
    local_y = np.where(lanes > cols, -1, lanes)
    keep_y = (lanes <= cols) | (lanes == cols + 127)
    inverse_y = np.stack(
        [
            real_basis(pair_y, sin_y, (h * cols + local_y) % length_y, length_y) * keep_y
            for h in range(groups_y)
        ]
    )
    kx = np.arange(length_x)
    pair_x = kx % (length_x // 2)
    sin_x = kx >= length_x // 2
    basis_x = real_basis(pair_x, sin_x, np.arange(length_x), length_x)
    forward_x = np.zeros((groups_x, 2, rows, 2, length_x))
    band = rows + 8
    inverse_x = np.zeros((2, length_x, groups_x, 128))
    local_x = np.arange(band)
    keep_x = (local_x <= rows) | (local_x == band - 1)
    local_x = np.where(local_x > rows, -1, local_x)
    for s in range(2):
        forward_x[:, s, :, s, :] = basis_x.T.reshape(groups_x, rows, length_x)
        for w in range(groups_x):
            part = basis_x[:, (w * rows + local_x) % length_x] * keep_x
            inverse_x[s, :, w, s * band : (s + 1) * band] = part
    forward_x = forward_x.reshape(groups_x, 2 * rows, 2 * length_x)
    inverse_x = inverse_x.reshape(2 * length_x, groups_x * 128)

    def halves(table, axis):
        coarse = table.astype(ml_dtypes.bfloat16)
        fine = (table - coarse.astype(np.float64)).astype(ml_dtypes.bfloat16)
        return np.stack([coarse, fine], axis=axis)

    forward_x = halves(forward_x, 1)
    forward_x = np.concatenate([forward_x[:, 0], forward_x[:, 0], forward_x[:, 1]], axis=1)
    return halves(forward_y, 1), halves(inverse_y, 1), forward_x, halves(inverse_x, 0)


def selectors():
    lift = np.zeros((2, 24), np.float32)
    taps = np.zeros((9, 24), np.float32)
    for a in range(3):
        for s in range(2):
            for b in range(3):
                lift[s, a * 8 + s * 3 + b] = 1.0
                taps[3 * a + b, a * 8 + s * 3 + b] = 1.0
    middle = np.zeros((32, 2), np.float32)
    middle[9, 0] = 1.0
    middle[12, 1] = 1.0
    return lift, taps, middle


def dot(a, b, dims=((1,), (0,)), exact=False):
    return lax.dot_general(
        a,
        b,
        (dims, ((), ())),
        precision=lax.Precision.HIGHEST if exact else None,
        preferred_element_type=jnp.float32,
    )


def put(ref, start, count, stride, value):
    for tile in range(ref.shape[0]):
        ref[tile, pl.ds(start, count, stride=stride), :] = value[:, tile * 128 : (tile + 1) * 128]


def take(ref, start, count, stride=1, tiles=None):
    rows = pl.ds(start, count, stride=stride)
    parts = [ref[tile, rows, :] for tile in range(tiles or ref.shape[0])]
    return jnp.concatenate(parts, axis=1)


def halved(value, axis):
    coarse = value.astype(jnp.bfloat16)
    fine = (value - coarse.astype(jnp.float32)).astype(jnp.bfloat16)
    return jnp.concatenate([coarse, fine], axis=axis)


def fused_kernel(
    groups_y,
    groups_x,
    rows,
    cols,
    vel_ref,
    cot_ref,
    lift_ref,
    taps_ref,
    point_ref,
    outw_ref,
    sel_lift_ref,
    sel_taps_ref,
    sel_mid_ref,
    fy_hbm,
    iy_hbm,
    fx_hbm,
    ix_hbm,
    gv_ref,
    glift_ref,
    gtaps_ref,
    gpoint_ref,
    gout_ref,
    fy,
    iy,
    fx,
    ix,
    gath,
    send2,
    recv2,
    send3,
    recv3,
    gath4,
    halo_out,
    halo_in,
    edge_out,
    edge_in,
    ext,
    shifts,
    tbuf,
    slope,
    gp2,
    ubuf,
    pay_y,
    pay_x,
    table_sem,
    s1,
    r1,
    s2,
    r2,
    s3,
    r3,
    s4,
    r4,
    sh,
    rh,
    se,
    re,
    s5,
    r5,
    s6,
    r6,
):
    bf16, f32 = jnp.bfloat16, jnp.float32
    h = lax.axis_index("ha")
    w = lax.axis_index("wa")
    length_x, length_y = groups_x * rows, groups_y * cols
    per = length_y // (groups_x * groups_y)
    half = per // 2
    wide = cols + 128
    band = rows + 8

    loads = [
        pltpu.make_async_copy(fy_hbm.at[h], fy, table_sem.at[0]),
        pltpu.make_async_copy(iy_hbm.at[h], iy, table_sem.at[1]),
        pltpu.make_async_copy(fx_hbm, fx, table_sem.at[2]),
        pltpu.make_async_copy(ix_hbm, ix, table_sem.at[3]),
    ]
    for load in (loads[0], loads[2], loads[3], loads[1]):
        load.start()

    def ha_peer(step):
        return lax.rem(h + step, groups_y)

    def wa_peer(step):
        return lax.rem(w + step, groups_x)

    barrier = pltpu.get_barrier_semaphore()
    for step in range(1, groups_y):
        pl.semaphore_signal(
            barrier, inc=1, device_id=(ha_peer(step), w), device_id_type=pl.DeviceIdType.MESH
        )
    for step in range(1, groups_x):
        pl.semaphore_signal(
            barrier, inc=1, device_id=(h, wa_peer(step)), device_id_type=pl.DeviceIdType.MESH
        )

    def remote(src, dst, send, recv, device):
        return pltpu.make_async_remote_copy(
            src_ref=src,
            dst_ref=dst,
            send_sem=send,
            recv_sem=recv,
            device_id=device,
            device_id_type=pl.DeviceIdType.MESH,
        )

    gath[h] = halved(cot_ref[...].reshape(2 * rows, cols), 0)
    vel = vel_ref[...].reshape(2 * rows, cols)
    halo_out[0] = vel[:, :128]
    halo_out[1] = vel[:, cols - 128 :]
    pl.semaphore_wait(barrier, groups_y + groups_x - 2)

    def spread_y(buf, send, recv):
        copies = []
        for step in range(1, groups_y):
            copy = remote(buf.at[h], buf.at[h], send.at[step], recv.at[h], (ha_peer(step), w))
            copy.start()
            copies.append(copy)
        return copies

    def arrived_y(buf, send, recv, step):
        src = ha_peer(step)
        remote(buf.at[src], buf.at[src], send.at[step], recv.at[src], (src, w)).wait_recv()
        return src

    def spread_x(src_of, buf, send, recv):
        copies = []
        for step in range(1, groups_x):
            dst = wa_peer(step)
            copy = remote(src_of(dst), buf.at[w], send.at[step], recv.at[w], (h, dst))
            copy.start()
            copies.append(copy)
        return copies

    def arrived_x(buf, send, recv, step):
        src = wa_peer(step)
        remote(buf.at[src], buf.at[src], send.at[step], recv.at[src], (h, src)).wait_recv()

    pending = spread_y(gath, s1, r1)
    left, right = (ha_peer(groups_y - 1), w), (ha_peer(1), w)
    halo = [
        remote(halo_out.at[0], halo_in.at[0], sh.at[0], rh.at[0], left),
        remote(halo_out.at[1], halo_in.at[1], sh.at[1], rh.at[1], right),
    ]
    for copy in halo:
        copy.start()

    lift_wide = dot(lift_ref[...], sel_lift_ref[...], exact=True)
    taps_wide = dot(taps_ref[0], sel_taps_ref[...], exact=True)
    both = lift_wide * taps_wide
    point = point_ref[0].astype(f32)
    mixed = dot(point, both, exact=True)
    coarse = mixed.astype(bf16).astype(f32)
    mixed_b = jnp.concatenate(
        [coarse, mixed - coarse, coarse, jnp.zeros_like(coarse[:, :8])], axis=1
    ).astype(bf16)
    none = jnp.zeros((8, wide), f32)
    outw = outw_ref[...].astype(f32)
    out_pad = jnp.concatenate([outw, jnp.zeros((14, outw.shape[1]), f32)], axis=0)
    out_b = out_pad.astype(bf16)
    through = dot(lift_ref[...], out_pad, ((0,), (1,)), exact=True)
    place = sel_mid_ref[...][:24]
    back_b = jnp.concatenate(
        [jnp.transpose(jnp.pad(mixed, ((0, 64), (0, 104))))[:24, :64], dot(place, through, exact=True)],
        axis=1,
    ).astype(bf16)

    row_id = lax.broadcasted_iota(jnp.int32, (per, length_x), 0)
    lane_id = lax.broadcasted_iota(jnp.int32, (per, length_x), 1)
    py = (h * groups_x + w) * half + lax.rem(row_id, half)
    px = lax.rem(lane_id, length_x // 2)
    ysin, xsin = row_id >= half, lane_id >= length_x // 2
    ky = jnp.where((py == 0) & ysin, length_y // 2, py).astype(f32)
    kx = jnp.where((px == 0) & xsin, length_x // 2, px).astype(f32)
    weight = jnp.where(py == 0, 1.0, 2.0) * jnp.where(px == 0, 1.0, 2.0) / (length_x * length_y)
    inverse_k = weight / jnp.maximum(kx * kx + ky * ky, 1.0)
    keep_0 = weight - kx * kx * inverse_k
    keep_1 = weight - ky * ky * inverse_k
    cross = kx * ky * inverse_k
    inner = (px != 0) & (py != 0)
    turn = jnp.where(inner, jnp.where(ysin == xsin, -cross, cross), 0.0)
    corner = jnp.where((px == 0) & (py == 0) & ysin & xsin, cross, 0.0)

    loads[0].wait()
    spec = jnp.zeros((cols, 2 * rows), f32)
    for step in range(groups_y):
        src = h if step == 0 else arrived_y(gath, s1, r1, step)
        where = pl.ds(pl.multiple_of(src * cols, cols), cols)
        field = gath[src]
        both_parts = dot(fy[0, :, where], field, ((1,), (1,)))
        spec = spec + both_parts[:, : 2 * rows] + both_parts[:, 2 * rows :]
        spec = spec + dot(fy[1, :, where], field[: 2 * rows], ((1,), (1,)))
    send2[...] = halved(spec, 1).reshape(groups_x, per, 4 * rows)
    pending += spread_x(lambda dst: send2.at[dst], recv2, s2, r2)
    recv2[w] = send2[w]

    for copy in halo:
        copy.wait()
    side = lax.broadcasted_iota(jnp.int32, (2 * rows, 128), 1)
    tail = jnp.where(side < 64, halo_in[0], halo_in[1])
    ext[:, :cols] = vel
    ext[:, cols:] = tail
    edge_out[...] = jnp.zeros_like(edge_out)
    for s in range(2):
        edge_out[0, 2 * s : 2 * s + 2, :] = ext[s * rows : s * rows + 2, :]
        edge_out[1, 2 * s : 2 * s + 2, :] = ext[s * rows + rows - 2 : s * rows + rows, :]
    edges = [
        remote(edge_out.at[0], edge_in.at[0], se.at[0], re.at[0], (h, wa_peer(groups_x - 1))),
        remote(edge_out.at[1], edge_in.at[1], se.at[1], re.at[1], (h, wa_peer(1))),
    ]
    for copy in edges:
        copy.start()
    shifts[...] = jnp.zeros_like(shifts)
    for s in range(2):
        for b in range(3):
            moved = ext[s * rows : (s + 1) * rows, :]
            if b != 1:
                moved = pltpu.roll(moved, (1 - b) % wide, 1)
            put(shifts, 16 + s * 3 + b, rows, 8, moved)

    loads[2].wait()
    for step in range(1, groups_x):
        arrived_x(recv2, s2, r2, step)
    waves = jnp.zeros((per, 2 * length_x), f32)
    for src in range(groups_x):
        got = recv2[src]
        waves = waves + dot(jnp.concatenate([got, got[:, : 2 * rows]], axis=1), fx[src])
    a0, a1 = waves[:, :length_x], waves[:, length_x:]

    def swapped(a):
        a = jnp.concatenate([a[half:], a[:half]], axis=0)
        return jnp.concatenate([a[:, length_x // 2 :], a[:, : length_x // 2]], axis=1)

    p0 = keep_0 * a0 - turn * swapped(a1) - corner * a1
    p1 = keep_1 * a1 - turn * swapped(a0) - corner * a0
    loads[3].wait()
    split = halved(jnp.concatenate([p0, p1], axis=1), 0)
    fields = dot(split, ix[0])
    fields = fields[:per] + fields[per:] + dot(split[:per], ix[1])
    for dst in range(groups_x):
        send3[dst] = fields[:, dst * 128 : (dst + 1) * 128]
    pending += spread_x(lambda dst: send3.at[dst], recv3, s3, r3)
    recv3[w] = send3[w]

    for copy in edges:
        copy.wait()
    for s in range(2):
        for b in range(3):
            for slot, first in ((1, 0), (0, rows + 2)):
                moved = edge_in[slot]
                if b != 1:
                    moved = pltpu.roll(moved, (1 - b) % wide, 1)
                for i in range(2):
                    at = 8 * (first + i) + s * 3 + b
                    put(shifts, at, 1, 1, moved[2 * s + i : 2 * s + i + 1])

    for step in range(1, groups_x):
        arrived_x(recv3, s3, r3, step)
    gath4[h] = halved(jnp.transpose(recv3[...].reshape(cols, 128))[: 2 * band], 0)
    pending += spread_y(gath4, s4, r4)

    def forward_row(i, carry):
        for j in range(2):
            n = 2 * i + j
            window = take(shifts, pl.multiple_of(8 * n, 8), 24)
            coarse = window.astype(bf16).astype(f32)
            window = jnp.concatenate([coarse, coarse, window - coarse, none], axis=0)
            tan = jnp.tanh(dot(mixed_b, window.astype(bf16)))
            tbuf[n] = tan.astype(bf16)
            slope[n] = (1.0 - tan * tan).astype(bf16)
        return carry

    lax.fori_loop(0, (rows + 2) // 2, forward_row, 0)

    loads[1].wait()
    field = jnp.zeros((2 * band, wide), f32)
    for step in range(groups_y):
        src = h if step == 0 else arrived_y(gath4, s4, r4, step)
        where = pl.ds(pl.multiple_of(src * cols, cols), cols)
        got = gath4[src]
        both_parts = dot(got, iy[0, where, :])
        field = field + both_parts[: 2 * band] + both_parts[2 * band :]
        field = field + dot(got[: 2 * band], iy[1, where, :])
    gp2[...] = jnp.zeros_like(gp2)
    for s in range(2):
        part = field[s * band : (s + 1) * band]
        put(gp2, 8 + s, rows, 8, part[:rows])
        put(gp2, 8 * (rows + 1) + s, 1, 1, part[rows : rows + 1])
        put(gp2, s, 1, 1, part[band - 1 :])

    def backward_row(n, own):
        gp8 = take(gp2, pl.multiple_of(8 * n, 8), 8)
        gp16 = jnp.concatenate([gp8, jnp.zeros_like(gp8)], axis=0).astype(bf16)
        tan = tbuf[n]
        gz = (dot(out_b, gp16, ((0,), (0,))) * slope[n].astype(f32)).astype(bf16)
        back = dot(back_b, jnp.concatenate([gz, gp16], axis=0))
        put(ubuf, pl.multiple_of(24 * n, 8), 24, 1, back)
        if not own:
            return None
        window = take(shifts, pl.multiple_of(8 * n, 8), 24, tiles=cols // 128)
        coarse = window.astype(bf16).astype(f32)
        pad = jnp.zeros_like(gp8[:, :cols])
        right_side = [window, gp8[:, :cols], window - coarse, pad]
        right_side = jnp.concatenate(right_side, axis=0).astype(bf16)
        left_side = jnp.concatenate([gz[:, :cols], tan[:, :cols], gp16[:, :cols]], axis=0)
        return dot(left_side, right_side, ((1,), (1,)))

    def backward_rows(i, total):
        for j in range(4):
            total = total + backward_row(1 + 4 * i + j, True)
        return total

    acc = lax.fori_loop(0, rows // 4, backward_rows, jnp.zeros((144, 64), f32))
    acc = acc[:, :32] + acc[:, 32:]

    low = lax.broadcasted_iota(jnp.int32, (64, 32), 1) < 24
    packed = jnp.concatenate(
        [jnp.where(low, acc[:64], acc[64:128]), acc[128:144], jnp.zeros((48, 32), f32)], axis=0
    )
    pay_y[h] = jnp.transpose(jnp.pad(packed, ((0, 0), (0, 96))))[:32]
    pending += spread_y(pay_y, s5, r5)

    backward_row(0, False)
    backward_row(rows + 1, False)
    for s in range(2):
        result = take(gp2, 8 + s, rows, 8)
        for b in range(3):
            k = s * 3 + b
            part = (
                take(ubuf, 48 + k, rows, 24)
                + take(ubuf, 24 + 8 + k, rows, 24)
                + take(ubuf, 16 + k, rows, 24)
            )
            if b != 1:
                part = pltpu.roll(part, (b - 1) % wide, 1)
            result = result + part
        gv_ref[s] = result[:, :cols]

    for step in range(1, groups_y):
        arrived_y(pay_y, s5, r5, step)
    summed = pay_y[0]
    for src in range(1, groups_y):
        summed = summed + pay_y[src]
    pay_x[w] = summed
    pending += spread_x(lambda dst: pay_x.at[w], pay_x, s6, r6)
    for step in range(1, groups_x):
        arrived_x(pay_x, s6, r6, step)
    sums = pay_x[0]
    for src in range(1, groups_x):
        sums = sums + pay_x[src]
    sums = sums * (1.0 / math.sqrt(length_x * length_y))
    turned = jnp.transpose(jnp.pad(sums, ((0, 96), (0, 0))))
    gz_sum = turned[:64, :24]
    pair = dot(turned[64:72, :32], sel_mid_ref[...], exact=True)[:2]
    depth = dot(point, gz_sum, ((0,), (0,)), exact=True)
    gpoint_ref[0] = dot(gz_sum, both, ((1,), (1,)), exact=True)
    gtaps_ref[0] = dot(depth * lift_wide, sel_taps_ref[...], ((1,), (1,)), exact=True)
    glift_ref[...] = dot(
        depth * taps_wide, sel_lift_ref[...], ((1,), (1,)), exact=True
    ) + dot(outw, pair, ((0,), (0,)), exact=True)
    gout_ref[...] = sums[24:26, :64] + dot(pair, lift_ref[...], ((1,), (1,)), exact=True)
    for copy in pending:
        copy.wait_send()


def fused(velocity, cotangent, lift_weight, depth_kernels, point_weights, out_weight):
    groups_y, groups_x = lax.axis_size("ha"), lax.axis_size("wa")
    _, rows, cols = velocity.shape
    channels = lift_weight.shape[0]
    length_x, length_y = groups_x * rows, groups_y * cols
    per = length_y // (groups_x * groups_y)
    wide = cols + 128
    tables = make_tables(groups_y, groups_x, rows, cols)
    bf16, f32 = jnp.bfloat16, jnp.float32
    vmem = pl.BlockSpec(memory_space=pltpu.VMEM)
    dma = pltpu.SemaphoreType.DMA
    return pl.pallas_call(
        functools.partial(fused_kernel, groups_y, groups_x, rows, cols),
        out_shape=(
            jax.ShapeDtypeStruct((2, rows, cols), f32),
            jax.ShapeDtypeStruct((channels, 2), f32),
            jax.ShapeDtypeStruct((1, channels, 9), f32),
            jax.ShapeDtypeStruct((1, channels, channels), f32),
            jax.ShapeDtypeStruct((2, channels), f32),
        ),
        in_specs=[vmem] * 9 + [pl.BlockSpec(memory_space=pl.ANY)] * 4,
        out_specs=(vmem,) * 5,
        scratch_shapes=[
            pltpu.VMEM((2, cols, length_y), bf16),
            pltpu.VMEM((2, length_y, wide), bf16),
            pltpu.VMEM((groups_x, 6 * rows, 2 * length_x), bf16),
            pltpu.VMEM((2, 2 * length_x, groups_x * 128), bf16),
            pltpu.VMEM((groups_y, 4 * rows, cols), bf16),
            pltpu.VMEM((groups_x, per, 4 * rows), bf16),
            pltpu.VMEM((groups_x, per, 4 * rows), bf16),
            pltpu.VMEM((groups_x, per, 128), f32),
            pltpu.VMEM((groups_x, per, 128), f32),
            pltpu.VMEM((groups_y, 4 * (rows + 8), cols), bf16),
            pltpu.VMEM((2, 2 * rows, 128), f32),
            pltpu.VMEM((2, 2 * rows, 128), f32),
            pltpu.VMEM((2, 8, wide), f32),
            pltpu.VMEM((2, 8, wide), f32),
            pltpu.VMEM((2 * rows, wide), f32),
            pltpu.VMEM((wide // 128, 8 * (rows + 4), 128), f32),
            pltpu.VMEM((rows + 2, channels, wide), bf16),
            pltpu.VMEM((rows + 2, channels, wide), bf16),
            pltpu.VMEM((wide // 128, 8 * (rows + 2), 128), f32),
            pltpu.VMEM((wide // 128, 24 * (rows + 2), 128), f32),
            pltpu.VMEM((groups_y, 32, 128), f32),
            pltpu.VMEM((groups_x, 32, 128), f32),
            dma((4,)),
            dma((groups_y,)),
            dma((groups_y,)),
            dma((groups_x,)),
            dma((groups_x,)),
            dma((groups_x,)),
            dma((groups_x,)),
            dma((groups_y,)),
            dma((groups_y,)),
            dma((2,)),
            dma((2,)),
            dma((2,)),
            dma((2,)),
            dma((groups_y,)),
            dma((groups_y,)),
            dma((groups_x,)),
            dma((groups_x,)),
        ],
        compiler_params=pltpu.CompilerParams(
            collective_id=0, has_side_effects=True, vmem_limit_bytes=48 * 1024 * 1024
        ),
    )(
        velocity,
        cotangent,
        lift_weight,
        depth_kernels,
        point_weights,
        out_weight,
        *[jnp.asarray(s) for s in selectors()],
        *[jnp.asarray(t) for t in tables],
    )


def either(velocity, cotangent, lift_weight, depth_kernels, point_weights, out_weight):
    groups_y, groups_x = lax.axis_size("ha"), lax.axis_size("wa")
    layers, channels, _ = depth_kernels.shape
    _, rows, cols = velocity.shape
    per = groups_y * cols // (groups_x * groups_y)
    fits = layers == 1 and channels == 64 and rows == 32 and cols % 256 == 0
    fits = fits and per % 32 == 0 and groups_y * cols <= 1024 and groups_x * rows == 256
    run = fused if fits else local
    return run(velocity, cotangent, lift_weight, depth_kernels, point_weights, out_weight)


def solution(mesh):
    return jax.shard_map(
        either,
        mesh=mesh,
        in_specs=(P(None, "wa", "ha"), P(None, "wa", "ha"), P(), P(), P(), P()),
        out_specs=(P(None, "wa", "ha"), P(), P(), P(), P()),
        check_vma=False,
    )
```

profile of v0, /device:TPU:0, one launch (start us, length us, event | category | flops | bytes accessed | tf_op | source)
XLA Modules:
  0.0 56.5 jit_solution(6231497158267700935)
XLA Ops:
  0.6 0.8 %copy.18.lift_ref = f32[64,2]{1,0:T(8,128)S(1)} copy(f32[64,2]{0,1:T(2,128)} %param.15) | data formatting | bytes 1024 | tf_op args[2]
  1.4 0.8 %copy.19.taps_ref = f32[1,64,9]{2,1,0:T(8,128)S(1)} copy(f32[1,64,9]{1,0,2:T(1,128)} %param.16) | data formatting | bytes 4608 | tf_op args[3]
  2.2 0.0 copy-start
  2.2 1.6 %copy-done = bf16[2,512,1024]{2,1,0:T(8,128)(2,1)S(1)} copy-done((bf16[2,512,1024]{2,1,0:T(8,128)(2,1)S(1)}, bf16[2,512,1024]{2,1,0:T(8,128)(2,1)}, u32[]{:S(2)}) %copy-start) | copy-done | bytes 2097176
  3.8 0.0 copy-start.1
  3.8 1.4 %copy-done.1 = bf16[8,192,512]{2,1,0:T(8,128)(2,1)S(1)} copy-done((bf16[8,192,512]{2,1,0:T(8,128)(2,1)S(1)}, bf16[8,192,512]{2,1,0:T(8,128)(2,1)}, u32[]{:S(2)}) %copy-start.1) | copy-done | bytes 1572888
  5.2 0.0 copy-start.2
  5.2 0.8 %copy-done.2 = f32[2,32,256]{2,1,0:T(8,128)S(1)} copy-done((f32[2,32,256]{2,1,0:T(8,128)S(1)}, f32[2,32,256]{2,1,0:T(8,128)}, u32[]{:S(2)}) %copy-start.2) | copy-done | bytes 65560
  6.0 0.0 copy-start.3
  6.0 0.8 %copy-done.3 = f32[2,32,256]{2,1,0:T(8,128)S(1)} copy-done((f32[2,32,256]{2,1,0:T(8,128)S(1)}, f32[2,32,256]{2,1,0:T(8,128)}, u32[]{:S(2)}) %copy-start.3) | copy-done | bytes 65560
  6.9 0.0 copy-start.4
  6.9 0.7 %copy-done.4 = bf16[1,64,64]{2,1,0:T(8,128)(2,1)S(1)} copy-done((bf16[1,64,64]{2,1,0:T(8,128)(2,1)S(1)}, bf16[1,64,64]{2,1,0:T(8,128)(2,1)}, u32[]{:S(2)}) %copy-start.4) | copy-done | bytes 8216
  7.6 0.0 copy-start.5
  7.6 0.7 %copy-done.5 = f32[32,2]{1,0:T(8,128)S(1)} copy-done((f32[32,2]{1,0:T(8,128)S(1)}, f32[32,2]{1,0:T(8,128)}, u32[]{:S(2)}) %copy-start.5) | copy-done | bytes 280
  8.3 0.0 copy-start.6
  8.3 0.7 %copy-done.6 = f32[9,24]{1,0:T(8,128)S(1)} copy-done((f32[9,24]{1,0:T(8,128)S(1)}, f32[9,24]{1,0:T(8,128)}, u32[]{:S(2)}) %copy-start.6) | copy-done | bytes 888
  9.0 0.0 copy-start.7
  9.0 0.7 %copy-done.7 = f32[2,24]{1,0:T(2,128)S(1)} copy-done((f32[2,24]{1,0:T(2,128)S(1)}, f32[2,24]{1,0:T(2,128)}, u32[]{:S(2)}) %copy-start.7) | copy-done | bytes 216
  9.7 0.0 copy-start.8
  9.7 0.7 %copy-done.8 = bf16[2,64]{1,0:T(2,128)(2,1)S(1)} copy-done((bf16[2,64]{1,0:T(2,128)(2,1)S(1)}, bf16[2,64]{1,0:T(2,128)(2,1)}, u32[]{:S(2)}) %copy-start.8) | copy-done | bytes 280
  10.3 43.1 %shard_map.164 = (f32[2,32,256]{2,1,0:T(8,128)S(1)}, f32[64,2]{1,0:T(8,128)S(1)}, f32[1,64,9]{2,1,0:T(8,128)S(1)}, f32[1,64,64]{2,1,0:T(8,128)S(1)}, f32[2,64]{1,0:T(2,128)S(1)}) custom-call(f32[2,32,256]{2,1,0:T(8,128)S(1)} %copy-done.2, f32[2,32,256]{2,1,0:T(8,128)S(1)} %copy-done.3, f32[64,2]{1,0:T(8,128)S(1)} %copy.18.lift_ref, ...), custom_call_target="tpu_custom_call" | custom-call | tf_op jit(solution)/shard_map/pallas_call | solution.py:709
  53.4 0.6 %copy.20 = f32[64,2]{0,1:T(2,128)} copy(f32[64,2]{1,0:T(8,128)S(1)} %get-tuple-element.6) | data formatting | bytes 1024 | tf_op jit(solution)/shard_map/pallas_call | solution.py:709
  54.1 0.7 %copy.21 = f32[1,64,9]{1,0,2:T(1,128)} copy(f32[1,64,9]{2,1,0:T(8,128)S(1)} %get-tuple-element.7) | data formatting | bytes 4608 | tf_op jit(solution)/shard_map/pallas_call | solution.py:709
  54.7 0.6 %copy.25 = f32[2,32,256]{2,1,0:T(8,128)} copy(f32[2,32,256]{2,1,0:T(8,128)S(1)} %get-tuple-element.15) | data formatting | bytes 131072
  55.3 0.6 %copy.26 = f32[1,64,64]{2,1,0:T(8,128)} copy(f32[1,64,64]{2,1,0:T(8,128)S(1)} %get-tuple-element.18) | data formatting | bytes 32768
  56.0 0.6 copy.27
Async XLA Ops:
  2.2 1.6 %copy-start = (bf16[2,512,1024]{2,1,0:T(8,128)(2,1)S(1)}, bf16[2,512,1024]{2,1,0:T(8,128)(2,1)}, u32[]{:S(2)}) copy-start(bf16[2,512,1024]{2,1,0:T(8,128)(2,1)} %constant.20.clone.ix_hbm) | copy-start | bytes 6291460
  3.8 1.4 %copy-start.1 = (bf16[8,192,512]{2,1,0:T(8,128)(2,1)S(1)}, bf16[8,192,512]{2,1,0:T(8,128)(2,1)}, u32[]{:S(2)}) copy-start(bf16[8,192,512]{2,1,0:T(8,128)(2,1)} %constant.19.clone.fx_hbm) | copy-start | bytes 4718596
  5.2 0.8 %copy-start.2 = (f32[2,32,256]{2,1,0:T(8,128)S(1)}, f32[2,32,256]{2,1,0:T(8,128)}, u32[]{:S(2)}) copy-start(f32[2,32,256]{2,1,0:T(8,128)} %vel_ref.1) | copy-start | bytes 196612
  6.0 0.8 %copy-start.3 = (f32[2,32,256]{2,1,0:T(8,128)S(1)}, f32[2,32,256]{2,1,0:T(8,128)}, u32[]{:S(2)}) copy-start(f32[2,32,256]{2,1,0:T(8,128)} %cot_ref.1) | copy-start | bytes 196612
  6.9 0.7 %copy-start.4 = (bf16[1,64,64]{2,1,0:T(8,128)(2,1)S(1)}, bf16[1,64,64]{2,1,0:T(8,128)(2,1)}, u32[]{:S(2)}) copy-start(bf16[1,64,64]{2,1,0:T(8,128)(2,1)} %point_ref.1) | copy-start | bytes 24580
  7.6 0.7 %copy-start.5 = (f32[32,2]{1,0:T(8,128)S(1)}, f32[32,2]{1,0:T(8,128)}, u32[]{:S(2)}) copy-start(f32[32,2]{1,0:T(8,128)} %constant.16.clone.sel_mid_ref) | copy-start | bytes 772
  8.3 0.7 %copy-start.6 = (f32[9,24]{1,0:T(8,128)S(1)}, f32[9,24]{1,0:T(8,128)}, u32[]{:S(2)}) copy-start(f32[9,24]{1,0:T(8,128)} %constant.15.clone.sel_taps_ref) | copy-start | bytes 2596
  9.0 0.7 %copy-start.7 = (f32[2,24]{1,0:T(2,128)S(1)}, f32[2,24]{1,0:T(2,128)}, u32[]{:S(2)}) copy-start(f32[2,24]{1,0:T(2,128)} %constant.14.clone.sel_lift_ref) | copy-start | bytes 580
  9.7 0.7 %copy-start.8 = (bf16[2,64]{1,0:T(2,128)(2,1)S(1)}, bf16[2,64]{1,0:T(2,128)(2,1)}, u32[]{:S(2)}) copy-start(bf16[2,64]{1,0:T(2,128)(2,1)} %outw_ref.1) | copy-start | bytes 772
where the time goes:
time: 57 us; the launch traced here: 56.5 us
  Pallas kernels  43.1 us (76%)
  local copies, waits for them, and re-layouts  12.8 us (22%)
  between operations  0.65 us (1%)
    pallas_call x1, Pallas kernels, fused(): pl.pallas_call(functools.partial(fused_kernel, groups_y, groups_x, rows,...  43.1 us
    unnamed x23, local copies, waits for them, and re-layouts  11.5 us
    pallas_call x2, local copies, waits for them, and re-layouts, fused(): pl.pallas_call(functools.partial(fused_kernel, groups_y, groups_x, rows,...  1.3 us

commit v1 on v0

--- a/solution.py
+++ b/solution.py
@@ -288,28 +288,8 @@
     return halves(forward_y, 1), halves(inverse_y, 1), forward_x, halves(inverse_x, 0)
 
 
-def selectors():
-    lift = np.zeros((2, 24), np.float32)
-    taps = np.zeros((9, 24), np.float32)
-    for a in range(3):
-        for s in range(2):
-            for b in range(3):
-                lift[s, a * 8 + s * 3 + b] = 1.0
-                taps[3 * a + b, a * 8 + s * 3 + b] = 1.0
-    middle = np.zeros((32, 2), np.float32)
-    middle[9, 0] = 1.0
-    middle[12, 1] = 1.0
-    return lift, taps, middle
-
-
-def dot(a, b, dims=((1,), (0,)), exact=False):
-    return lax.dot_general(
-        a,
-        b,
-        (dims, ((), ())),
-        precision=lax.Precision.HIGHEST if exact else None,
-        preferred_element_type=jnp.float32,
-    )
+def dot(a, b, dims=((1,), (0,))):
+    return lax.dot_general(a, b, (dims, ((), ())), preferred_element_type=jnp.float32)
 
 
 def put(ref, start, count, stride, value):
@@ -334,15 +314,12 @@
     groups_x,
     rows,
     cols,
-    vel_ref,
-    cot_ref,
-    lift_ref,
-    taps_ref,
-    point_ref,
-    outw_ref,
-    sel_lift_ref,
-    sel_taps_ref,
-    sel_mid_ref,
+    vel_hbm,
+    cot_hbm,
+    lift_hbm,
+    taps_hbm,
+    point_hbm,
+    outw_hbm,
     fy_hbm,
     iy_hbm,
     fx_hbm,
@@ -352,6 +329,12 @@
     gtaps_ref,
     gpoint_ref,
     gout_ref,
+    vel_ref,
+    cot_ref,
+    lift_ref,
+    taps_ref,
+    point_ref,
+    outw_ref,
     fy,
     iy,
     fx,
@@ -407,7 +390,18 @@
         pltpu.make_async_copy(fx_hbm, fx, table_sem.at[2]),
         pltpu.make_async_copy(ix_hbm, ix, table_sem.at[3]),
     ]
-    for load in (loads[0], loads[2], loads[3], loads[1]):
+    pairs = [
+        (cot_hbm, cot_ref),
+        (vel_hbm, vel_ref),
+        (lift_hbm, lift_ref),
+        (taps_hbm, taps_ref),
+        (point_hbm, point_ref),
+        (outw_hbm, outw_ref),
+    ]
+    small = [
+        pltpu.make_async_copy(src, dst, table_sem.at[4 + i]) for i, (src, dst) in enumerate(pairs)
+    ]
+    for load in small + [loads[0], loads[2], loads[3], loads[1]]:
         load.start()
 
     def ha_peer(step):
@@ -436,7 +430,9 @@
             device_id_type=pl.DeviceIdType.MESH,
         )
 
+    small[0].wait()
     gath[h] = halved(cot_ref[...].reshape(2 * rows, cols), 0)
+    small[1].wait()
     vel = vel_ref[...].reshape(2 * rows, cols)
     halo_out[0] = vel[:, :128]
     halo_out[1] = vel[:, cols - 128 :]
@@ -467,6 +463,7 @@
     def arrived_x(buf, send, recv, step):
         src = wa_peer(step)
         remote(buf.at[src], buf.at[src], send.at[step], recv.at[src], (h, src)).wait_recv()
+        return src
 
     pending = spread_y(gath, s1, r1)
     left, right = (ha_peer(groups_y - 1), w), (ha_peer(1), w)
@@ -477,25 +474,40 @@
     for copy in halo:
         copy.start()
 
-    lift_wide = dot(lift_ref[...], sel_lift_ref[...], exact=True)
-    taps_wide = dot(taps_ref[0], sel_taps_ref[...], exact=True)
+    for load in small[2:]:
+        load.wait()
+    lift = lift_ref[...]
+    taps = taps_ref[:, 0, :]
+    point = point_ref[0]
+    outw = outw_ref[...].astype(f32)
+    empty = jnp.zeros((2, lift.shape[1]), f32)
+    lift_wide, taps_wide = [], []
+    for a in range(3):
+        for k in range(2):
+            lift_wide += [lift[k : k + 1]] * 3
+            taps_wide += [taps[3 * a : 3 * a + 3]]
+        lift_wide.append(empty)
+        taps_wide.append(empty)
+    lift_wide = jnp.concatenate(lift_wide, axis=0)
+    taps_wide = jnp.concatenate(taps_wide, axis=0)
     both = lift_wide * taps_wide
-    point = point_ref[0].astype(f32)
-    mixed = dot(point, both, exact=True)
+    mixed = dot(halved(both, 0), point, ((1,), (1,)))
+    mixed = mixed[:24] + mixed[24:]
     coarse = mixed.astype(bf16).astype(f32)
-    mixed_b = jnp.concatenate(
-        [coarse, mixed - coarse, coarse, jnp.zeros_like(coarse[:, :8])], axis=1
-    ).astype(bf16)
+    stack = [coarse, mixed - coarse, coarse, jnp.zeros((56, 64), f32)]
+    stack = jnp.pad(jnp.concatenate(stack, axis=0), ((0, 0), (0, 64)))
+    mixed_b = jnp.transpose(stack)[:64, :80].astype(bf16)
     none = jnp.zeros((8, wide), f32)
-    outw = outw_ref[...].astype(f32)
-    out_pad = jnp.concatenate([outw, jnp.zeros((14, outw.shape[1]), f32)], axis=0)
-    out_b = out_pad.astype(bf16)
-    through = dot(lift_ref[...], out_pad, ((0,), (1,)), exact=True)
-    place = sel_mid_ref[...][:24]
-    back_b = jnp.concatenate(
-        [jnp.transpose(jnp.pad(mixed, ((0, 64), (0, 104))))[:24, :64], dot(place, through, exact=True)],
-        axis=1,
-    ).astype(bf16)
+    out_pad = jnp.concatenate([outw, jnp.zeros((14, 64), f32)], axis=0)
+    columns = jnp.transpose(jnp.pad(out_pad, ((0, 112), (0, 64))))
+    out_0 = jnp.broadcast_to(columns[:64, 0:1], (64, wide))
+    out_1 = jnp.broadcast_to(columns[:64, 1:2], (64, wide))
+    lift_pad = jnp.concatenate([lift, jnp.zeros((6, 64), f32)], axis=0)
+    through = dot(halved(lift_pad, 0), out_pad.astype(bf16), ((1,), (1,)))
+    through = through[:8] + through[8:]
+    row_24 = lax.broadcasted_iota(jnp.int32, (24, 16), 0)
+    place = jnp.where(row_24 == 9, through[0:1], jnp.where(row_24 == 12, through[1:2], 0.0))
+    back_b = jnp.concatenate([mixed, place], axis=1).astype(bf16)
 
     row_id = lax.broadcasted_iota(jnp.int32, (per, length_x), 0)
     lane_id = lax.broadcasted_iota(jnp.int32, (per, length_x), 1)
@@ -551,10 +563,9 @@
             put(shifts, 16 + s * 3 + b, rows, 8, moved)
 
     loads[2].wait()
-    for step in range(1, groups_x):
-        arrived_x(recv2, s2, r2, step)
     waves = jnp.zeros((per, 2 * length_x), f32)
-    for src in range(groups_x):
+    for step in range(groups_x):
+        src = w if step == 0 else arrived_x(recv2, s2, r2, step)
         got = recv2[src]
         waves = waves + dot(jnp.concatenate([got, got[:, : 2 * rows]], axis=1), fx[src])
     a0, a1 = waves[:, :length_x], waves[:, length_x:]
@@ -624,7 +635,9 @@
         gp8 = take(gp2, pl.multiple_of(8 * n, 8), 8)
         gp16 = jnp.concatenate([gp8, jnp.zeros_like(gp8)], axis=0).astype(bf16)
         tan = tbuf[n]
-        gz = (dot(out_b, gp16, ((0,), (0,))) * slope[n].astype(f32)).astype(bf16)
+        gpb = gp16.astype(f32)
+        grad = out_0 * gpb[0:1] + out_1 * gpb[1:2]
+        gz = (grad * slope[n].astype(f32)).astype(bf16)
         back = dot(back_b, jnp.concatenate([gz, gp16], axis=0))
         put(ubuf, pl.multiple_of(24 * n, 8), 24, 1, back)
         if not own:
@@ -681,16 +694,33 @@
     for src in range(1, groups_x):
         sums = sums + pay_x[src]
     sums = sums * (1.0 / math.sqrt(length_x * length_y))
-    turned = jnp.transpose(jnp.pad(sums, ((0, 96), (0, 0))))
-    gz_sum = turned[:64, :24]
-    pair = dot(turned[64:72, :32], sel_mid_ref[...], exact=True)[:2]
-    depth = dot(point, gz_sum, ((0,), (0,)), exact=True)
-    gpoint_ref[0] = dot(gz_sum, both, ((1,), (1,)), exact=True)
-    gtaps_ref[0] = dot(depth * lift_wide, sel_taps_ref[...], ((1,), (1,)), exact=True)
-    glift_ref[...] = dot(
-        depth * taps_wide, sel_lift_ref[...], ((1,), (1,)), exact=True
-    ) + dot(outw, pair, ((0,), (0,)), exact=True)
-    gout_ref[...] = sums[24:26, :64] + dot(pair, lift_ref[...], ((1,), (1,)), exact=True)
+    gz_sum = sums[:24, :64]
+    depth = dot(halved(gz_sum, 0), point)
+    depth = depth[:24] + depth[24:]
+    fine = gz_sum - gz_sum.astype(bf16).astype(f32)
+    left_side = jnp.concatenate([gz_sum, fine, gz_sum, jnp.zeros((56, 64), f32)], axis=0)
+    left_side = jnp.transpose(jnp.pad(left_side, ((0, 0), (0, 64))))[:64, :80].astype(bf16)
+    fine = both - both.astype(bf16).astype(f32)
+    right_side = jnp.concatenate([both, both, fine, jnp.zeros((8, 64), f32)], axis=0).astype(bf16)
+    gpoint_ref[0] = dot(left_side, right_side)
+    by_tap = depth * lift_wide
+    by_lift = depth * taps_wide
+    for a in range(3):
+        for b in range(3):
+            k = 8 * a + b
+            gtaps_ref[3 * a + b] = by_tap[k : k + 1] + by_tap[k + 3 : k + 4]
+    for s in range(2):
+        total = jnp.zeros((1, 64), f32)
+        for a in range(3):
+            k = 8 * a + 3 * s
+            total = total + jnp.sum(by_lift[k : k + 3], axis=0, keepdims=True)
+        for r in range(2):
+            total = total + sums[9 + 3 * s : 10 + 3 * s, 64 + r : 65 + r] * outw[r : r + 1]
+        glift_ref[s : s + 1] = total
+        total = sums[24 + s : 25 + s, :64]
+        for r in range(2):
+            total = total + sums[9 + 3 * r : 10 + 3 * r, 64 + s : 65 + s] * lift[r : r + 1]
+        gout_ref[s : s + 1] = total
     for copy in pending:
         copy.wait_send()
 
@@ -706,18 +736,24 @@
     bf16, f32 = jnp.bfloat16, jnp.float32
     vmem = pl.BlockSpec(memory_space=pltpu.VMEM)
     dma = pltpu.SemaphoreType.DMA
-    return pl.pallas_call(
+    results = pl.pallas_call(
         functools.partial(fused_kernel, groups_y, groups_x, rows, cols),
         out_shape=(
             jax.ShapeDtypeStruct((2, rows, cols), f32),
-            jax.ShapeDtypeStruct((channels, 2), f32),
-            jax.ShapeDtypeStruct((1, channels, 9), f32),
+            jax.ShapeDtypeStruct((2, channels), f32),
+            jax.ShapeDtypeStruct((9, 1, channels), f32),
             jax.ShapeDtypeStruct((1, channels, channels), f32),
             jax.ShapeDtypeStruct((2, channels), f32),
         ),
-        in_specs=[vmem] * 9 + [pl.BlockSpec(memory_space=pl.ANY)] * 4,
+        in_specs=[pl.BlockSpec(memory_space=pltpu.HBM)] * 10,
         out_specs=(vmem,) * 5,
         scratch_shapes=[
+            pltpu.VMEM((2, rows, cols), f32),
+            pltpu.VMEM((2, rows, cols), f32),
+            pltpu.VMEM((2, channels), f32),
+            pltpu.VMEM((9, 1, channels), f32),
+            pltpu.VMEM((1, channels, channels), bf16),
+            pltpu.VMEM((2, channels), bf16),
             pltpu.VMEM((2, cols, length_y), bf16),
             pltpu.VMEM((2, length_y, wide), bf16),
             pltpu.VMEM((groups_x, 6 * rows, 2 * length_x), bf16),
@@ -740,7 +776,7 @@
             pltpu.VMEM((wide // 128, 24 * (rows + 2), 128), f32),
             pltpu.VMEM((groups_y, 32, 128), f32),
             pltpu.VMEM((groups_x, 32, 128), f32),
-            dma((4,)),
+            dma((10,)),
             dma((groups_y,)),
             dma((groups_y,)),
             dma((groups_x,)),
@@ -759,18 +795,19 @@
             dma((groups_x,)),
         ],
         compiler_params=pltpu.CompilerParams(
-            collective_id=0, has_side_effects=True, vmem_limit_bytes=48 * 1024 * 1024
+            collective_id=0, has_side_effects=True, vmem_limit_bytes=64 * 1024 * 1024
         ),
     )(
         velocity,
         cotangent,
-        lift_weight,
-        depth_kernels,
+        lift_weight.T,
+        jnp.transpose(depth_kernels, (2, 0, 1)),
         point_weights,
         out_weight,
-        *[jnp.asarray(s) for s in selectors()],
         *[jnp.asarray(t) for t in tables],
     )
+    grad_velocity, grad_lift, grad_taps, grad_point, grad_out = results
+    return grad_velocity, grad_lift.T, jnp.transpose(grad_taps, (1, 2, 0)), grad_point, grad_out
 
 
 def either(velocity, cotangent, lift_weight, depth_kernels, point_weights, out_weight):

time: 57 us -> 46.6 us (0.82)
  local copies, waits for them, and re-layouts: 12.8 us -> 6.58 us
  Pallas kernels: 43.1 us -> 39.1 us
    unnamed x23 -> x5, local copies, waits for them, and re-layouts: 11.5 us -> 6.58 us
    pallas_call x1, Pallas kernels: 43.1 us -> 39.1 us  [fused(): pl.pallas_call(functools.partial(fused_kernel, groups_y, groups_x, rows,...]
    pallas_call x2 -> x0, local copies, waits for them, and re-layouts: 1.3 us -> none  [fused(): pl.pallas_call(functools.partial(fused_kernel, groups_y, groups_x, rows,...]
where the time goes in v1:
time: 46.6 us; the launch traced here: 46.3 us
  Pallas kernels  39.1 us (84%)
  local copies, waits for them, and re-layouts  6.58 us (14%)
  between operations  0.64 us (1%)
    pallas_call x1, Pallas kernels, fused(): pl.pallas_call(functools.partial(fused_kernel, groups_y, groups_x, rows,...  39.1 us
    unnamed x5, local copies, waits for them, and re-layouts  6.58 us

profile of v1, /device:TPU:0, one launch (start us, length us, event | category | flops | bytes accessed | tf_op | source)
XLA Modules:
  0.0 46.3 jit_solution(12377938566725158368)
XLA Ops:
  0.6 39.1 %shard_map.137 = (f32[2,32,256]{2,1,0:T(8,128)}, f32[2,64]{1,0:T(2,128)}, f32[9,1,64]{2,1,0:T(1,128)}, f32[1,64,64]{2,1,0:T(8,128)}, f32[2,64]{1,0:T(2,128)}) custom-call(f32[2,32,256]{2,1,0:T(8,128)} %vel_hbm.1, f32[2,32,256]{2,1,0:T(8,128)} %cot_hbm.1, f32[2,64]{1,0:T(2,128)} %bitcast.6, f32[9,1,64]{2,1,0:T(1,128)} %bitcast.4, ...), custom_call_target="tpu_custom_call" | custom-call | tf_op jit(solution)/shard_map/pallas_call | solution.py:739
  39.7 1.5 %copy.20 = f32[2,32,256]{2,1,0:T(8,128)} copy(f32[2,32,256]{2,1,0:T(8,128)} %get-tuple-element.20) | data formatting | bytes 131072
  41.2 1.2 %copy.21 = f32[64,2]{0,1:T(2,128)} copy(f32[64,2]{0,1:T(2,128)} %bitcast.7) | data formatting | bytes 1024
  42.4 1.3 %copy.22 = f32[1,64,9]{1,0,2:T(1,128)} copy(f32[1,64,9]{1,0,2:T(1,128)} %bitcast.5) | data formatting | bytes 4608
  43.7 1.4 %copy.23 = f32[1,64,64]{2,1,0:T(8,128)} copy(f32[1,64,64]{2,1,0:T(8,128)} %get-tuple-element.23) | data formatting | bytes 32768
  45.1 1.2 %copy.24 = f32[2,64]{1,0:T(2,128)} copy(f32[2,64]{1,0:T(2,128)} %get-tuple-element.24) | data formatting | bytes 1024

commit v2 on v1

--- a/solution.py
+++ b/solution.py
@@ -562,6 +562,25 @@
                 moved = pltpu.roll(moved, (1 - b) % wide, 1)
             put(shifts, 16 + s * 3 + b, rows, 8, moved)
 
+    def forward_row(n):
+        start = n * 8 if isinstance(n, int) else pl.multiple_of(8 * n, 8)
+        window = take(shifts, start, 24)
+        coarse = window.astype(bf16).astype(f32)
+        window = jnp.concatenate([coarse, coarse, window - coarse, none], axis=0)
+        tan = jnp.tanh(dot(mixed_b, window.astype(bf16)))
+        tbuf[n] = tan.astype(bf16)
+        slope[n] = (1.0 - tan * tan).astype(bf16)
+
+    def forward_rows(first, count):
+        def two(i, carry):
+            forward_row(first + 2 * i)
+            forward_row(first + 2 * i + 1)
+            return carry
+
+        lax.fori_loop(0, count // 2, two, 0)
+
+    forward_rows(2, 4)
+
     loads[2].wait()
     waves = jnp.zeros((per, 2 * length_x), f32)
     for step in range(groups_x):
@@ -579,12 +598,13 @@
     loads[3].wait()
     split = halved(jnp.concatenate([p0, p1], axis=1), 0)
     fields = dot(split, ix[0])
-    fields = fields[:per] + fields[per:] + dot(split[:per], ix[1])
+    fields = (fields[:per] + fields[per:] + dot(split[:per], ix[1])).astype(bf16)
     for dst in range(groups_x):
         send3[dst] = fields[:, dst * 128 : (dst + 1) * 128]
     pending += spread_x(lambda dst: send3.at[dst], recv3, s3, r3)
     recv3[w] = send3[w]
 
+    forward_rows(6, 10)
     for copy in edges:
         copy.wait()
     for s in range(2):
@@ -599,31 +619,20 @@
 
     for step in range(1, groups_x):
         arrived_x(recv3, s3, r3, step)
-    gath4[h] = halved(jnp.transpose(recv3[...].reshape(cols, 128))[: 2 * band], 0)
+    turned = jnp.transpose(recv3[...].reshape(cols, 128).astype(f32))
+    gath4[h] = turned[: 2 * band].astype(bf16)
     pending += spread_y(gath4, s4, r4)
 
-    def forward_row(i, carry):
-        for j in range(2):
-            n = 2 * i + j
-            window = take(shifts, pl.multiple_of(8 * n, 8), 24)
-            coarse = window.astype(bf16).astype(f32)
-            window = jnp.concatenate([coarse, coarse, window - coarse, none], axis=0)
-            tan = jnp.tanh(dot(mixed_b, window.astype(bf16)))
-            tbuf[n] = tan.astype(bf16)
-            slope[n] = (1.0 - tan * tan).astype(bf16)
-        return carry
-
-    lax.fori_loop(0, (rows + 2) // 2, forward_row, 0)
-
+    forward_rows(16, rows - 16)
+    for n in (0, 1, rows, rows + 1):
+        forward_row(n)
     loads[1].wait()
     field = jnp.zeros((2 * band, wide), f32)
     for step in range(groups_y):
         src = h if step == 0 else arrived_y(gath4, s4, r4, step)
         where = pl.ds(pl.multiple_of(src * cols, cols), cols)
         got = gath4[src]
-        both_parts = dot(got, iy[0, where, :])
-        field = field + both_parts[: 2 * band] + both_parts[2 * band :]
-        field = field + dot(got[: 2 * band], iy[1, where, :])
+        field = field + dot(got, iy[0, where, :]) + dot(got, iy[1, where, :])
     gp2[...] = jnp.zeros_like(gp2)
     for s in range(2):
         part = field[s * band : (s + 1) * band]
@@ -662,7 +671,10 @@
     packed = jnp.concatenate(
         [jnp.where(low, acc[:64], acc[64:128]), acc[128:144], jnp.zeros((48, 32), f32)], axis=0
     )
-    pay_y[h] = jnp.transpose(jnp.pad(packed, ((0, 0), (0, 96))))[:32]
+    packed = jnp.transpose(jnp.pad(packed, ((0, 0), (0, 96))))[:32]
+    upper = [packed[16:26, :64], packed[9:10, 64:], packed[12:13, 64:], packed[28:32, :64]]
+    upper = jnp.concatenate(upper, axis=0)
+    pay_y[h] = jnp.concatenate([packed[:16, :64], upper], axis=1)
     pending += spread_y(pay_y, s5, r5)
 
     backward_row(0, False)
@@ -694,7 +706,7 @@
     for src in range(1, groups_x):
         sums = sums + pay_x[src]
     sums = sums * (1.0 / math.sqrt(length_x * length_y))
-    gz_sum = sums[:24, :64]
+    gz_sum = jnp.concatenate([sums[:, :64], sums[:8, 64:]], axis=0)
     depth = dot(halved(gz_sum, 0), point)
     depth = depth[:24] + depth[24:]
     fine = gz_sum - gz_sum.astype(bf16).astype(f32)
@@ -715,14 +727,23 @@
             k = 8 * a + 3 * s
             total = total + jnp.sum(by_lift[k : k + 3], axis=0, keepdims=True)
         for r in range(2):
-            total = total + sums[9 + 3 * s : 10 + 3 * s, 64 + r : 65 + r] * outw[r : r + 1]
+            total = total + sums[10 + s : 11 + s, 64 + r : 65 + r] * outw[r : r + 1]
         glift_ref[s : s + 1] = total
-        total = sums[24 + s : 25 + s, :64]
+        total = sums[8 + s : 9 + s, 64:]
         for r in range(2):
-            total = total + sums[9 + 3 * r : 10 + 3 * r, 64 + s : 65 + s] * lift[r : r + 1]
+            total = total + sums[10 + r : 11 + r, 64 + s : 65 + s] * lift[r : r + 1]
         gout_ref[s : s + 1] = total
     for copy in pending:
         copy.wait_send()
+
+
+def hand_over(*refs):
+    sources, targets, sems = refs[:5], refs[5:10], refs[10]
+    copies = [pltpu.make_async_copy(sources[i], targets[i], sems.at[i]) for i in range(5)]
+    for copy in copies:
+        copy.start()
+    for copy in copies:
+        copy.wait()
 
 
 def fused(velocity, cotangent, lift_weight, depth_kernels, point_weights, out_weight):
@@ -761,9 +782,9 @@
             pltpu.VMEM((groups_y, 4 * rows, cols), bf16),
             pltpu.VMEM((groups_x, per, 4 * rows), bf16),
             pltpu.VMEM((groups_x, per, 4 * rows), bf16),
-            pltpu.VMEM((groups_x, per, 128), f32),
-            pltpu.VMEM((groups_x, per, 128), f32),
-            pltpu.VMEM((groups_y, 4 * (rows + 8), cols), bf16),
+            pltpu.VMEM((groups_x, per, 128), bf16),
+            pltpu.VMEM((groups_x, per, 128), bf16),
+            pltpu.VMEM((groups_y, 2 * (rows + 8), cols), bf16),
             pltpu.VMEM((2, 2 * rows, 128), f32),
             pltpu.VMEM((2, 2 * rows, 128), f32),
             pltpu.VMEM((2, 8, wide), f32),
@@ -774,8 +795,8 @@
             pltpu.VMEM((rows + 2, channels, wide), bf16),
             pltpu.VMEM((wide // 128, 8 * (rows + 2), 128), f32),
             pltpu.VMEM((wide // 128, 24 * (rows + 2), 128), f32),
-            pltpu.VMEM((groups_y, 32, 128), f32),
-            pltpu.VMEM((groups_x, 32, 128), f32),
+            pltpu.VMEM((groups_y, 16, 128), f32),
+            pltpu.VMEM((groups_x, 16, 128), f32),
             dma((10,)),
             dma((groups_y,)),
             dma((groups_y,)),
@@ -806,6 +827,14 @@
         out_weight,
         *[jnp.asarray(t) for t in tables],
     )
+    results = pl.pallas_call(
+        hand_over,
+        out_shape=[jax.ShapeDtypeStruct(r.shape, r.dtype) for r in results],
+        in_specs=[pl.BlockSpec(memory_space=pltpu.HBM)] * 5,
+        out_specs=[pl.BlockSpec(memory_space=pltpu.HBM)] * 5,
+        scratch_shapes=[dma((5,))],
+        compiler_params=pltpu.CompilerParams(vmem_limit_bytes=64 * 1024 * 1024),
+    )(*results)
     grad_velocity, grad_lift, grad_taps, grad_point, grad_out = results
     return grad_velocity, grad_lift.T, jnp.transpose(grad_taps, (1, 2, 0)), grad_point, grad_out
 

time: 46.6 us -> 40.6 us (0.87)
  local copies, waits for them, and re-layouts: 6.58 us -> 0 us
  Pallas kernels: 39.1 us -> 39.8 us
    unnamed x5 -> x0, local copies, waits for them, and re-layouts: 6.58 us -> none
    pallas_call x0 -> x1, Pallas kernels: none -> 4.33 us  [fused(): pl.pallas_call(hand_over, out_shape=[jax.ShapeDtypeStruct(r.shape, r.dtyp...]
    pallas_call x1, Pallas kernels: 39.1 us -> 35.5 us  [fused(): pl.pallas_call(functools.partial(fused_kernel, groups_y, groups_x, rows,...]
where the time goes in v2:
time: 40.6 us; the launch traced here: 40.4 us
  Pallas kernels  39.8 us (98%)
  between operations  0.64 us (2%)
    pallas_call x1, Pallas kernels, fused(): pl.pallas_call(functools.partial(fused_kernel, groups_y, groups_x, rows,...  35.5 us
    pallas_call x1, Pallas kernels, fused(): pl.pallas_call(hand_over, out_shape=[jax.ShapeDtypeStruct(r.shape, r.dtyp...  4.33 us

profile of v2, /device:TPU:0, one launch (start us, length us, event | category | flops | bytes accessed | tf_op | source)
XLA Modules:
  0.0 40.4 jit_solution(1946758970935164055)
XLA Ops:
  0.6 35.5 %shard_map.137 = (f32[2,32,256]{2,1,0:T(8,128)}, f32[2,64]{1,0:T(2,128)}, f32[9,1,64]{2,1,0:T(1,128)}, f32[1,64,64]{2,1,0:T(8,128)}, f32[2,64]{1,0:T(2,128)}) custom-call(f32[2,32,256]{2,1,0:T(8,128)} %vel_hbm.1, f32[2,32,256]{2,1,0:T(8,128)} %cot_hbm.1, f32[2,64]{1,0:T(2,128)} %bitcast.5, f32[9,1,64]{2,1,0:T(1,128)} %bitcast.4, ...), custom_call_target="tpu_custom_call" | custom-call | tf_op jit(solution)/shard_map/pallas_call | solution.py:760
  36.1 4.3 %shard_map.138 = (f32[2,32,256]{2,1,0:T(8,128)}, f32[2,64]{1,0:T(2,128)}, f32[9,1,64]{2,1,0:T(1,128)}, f32[1,64,64]{2,1,0:T(8,128)}, f32[2,64]{1,0:T(2,128)}) custom-call(f32[2,32,256]{2,1,0:T(8,128)} %get-tuple-element.15.refs_0_, f32[2,64]{1,0:T(2,128)} %get-tuple-element.16.refs_1_, f32[9,1,64]{2,1,0:T(1,128)} %get-tuple-element.17.refs_2_, ...), custom_call_target="tpu_custom_call" | custom-call | tf_op jit(solution)/shard_map/pallas_call | solution.py:830

commit v3 on v2

--- a/solution.py
+++ b/solution.py
@@ -309,6 +309,18 @@
     return jnp.concatenate([coarse, fine], axis=axis)
 
 
+def widened(lift, taps):
+    empty = jnp.zeros((2, lift.shape[1]), jnp.float32)
+    lift_wide, taps_wide = [], []
+    for a in range(3):
+        for k in range(2):
+            lift_wide += [lift[k : k + 1]] * 3
+            taps_wide += [taps[3 * a : 3 * a + 3]]
+        lift_wide.append(empty)
+        taps_wide.append(empty)
+    return jnp.concatenate(lift_wide, axis=0), jnp.concatenate(taps_wide, axis=0)
+
+
 def fused_kernel(
     groups_y,
     groups_x,
@@ -324,11 +336,10 @@
     iy_hbm,
     fx_hbm,
     ix_hbm,
+    gv_hbm,
+    sums_hbm,
     gv_ref,
-    glift_ref,
-    gtaps_ref,
-    gpoint_ref,
-    gout_ref,
+    sums_ref,
     vel_ref,
     cot_ref,
     lift_ref,
@@ -480,16 +491,7 @@
     taps = taps_ref[:, 0, :]
     point = point_ref[0]
     outw = outw_ref[...].astype(f32)
-    empty = jnp.zeros((2, lift.shape[1]), f32)
-    lift_wide, taps_wide = [], []
-    for a in range(3):
-        for k in range(2):
-            lift_wide += [lift[k : k + 1]] * 3
-            taps_wide += [taps[3 * a : 3 * a + 3]]
-        lift_wide.append(empty)
-        taps_wide.append(empty)
-    lift_wide = jnp.concatenate(lift_wide, axis=0)
-    taps_wide = jnp.concatenate(taps_wide, axis=0)
+    lift_wide, taps_wide = widened(lift, taps)
     both = lift_wide * taps_wide
     mixed = dot(halved(both, 0), point, ((1,), (1,)))
     mixed = mixed[:24] + mixed[24:]
@@ -692,6 +694,8 @@
                 part = pltpu.roll(part, (b - 1) % wide, 1)
             result = result + part
         gv_ref[s] = result[:, :cols]
+    leave_gv = pltpu.make_async_copy(gv_ref, gv_hbm, table_sem.at[10])
+    leave_gv.start()
 
     for step in range(1, groups_y):
         arrived_y(pay_y, s5, r5, step)
@@ -706,6 +710,66 @@
     for src in range(1, groups_x):
         sums = sums + pay_x[src]
     sums = sums * (1.0 / math.sqrt(length_x * length_y))
+    sums_ref[...] = sums
+    leave = pltpu.make_async_copy(sums_ref, sums_hbm, table_sem.at[11])
+    leave.start()
+    for copy in pending:
+        copy.wait_send()
+    leave_gv.wait()
+    leave.wait()
+
+
+def finish_kernel(
+    gv_in,
+    sums_hbm,
+    lift_hbm,
+    taps_hbm,
+    point_hbm,
+    outw_hbm,
+    gv_out,
+    lift_out,
+    taps_out,
+    point_out,
+    out_out,
+    sums_ref,
+    lift_ref,
+    taps_ref,
+    point_ref,
+    outw_ref,
+    glift_ref,
+    gtaps_ref,
+    gpoint_ref,
+    gout_ref,
+    sem,
+):
+    bf16, f32 = jnp.bfloat16, jnp.float32
+    pairs = [
+        (sums_hbm, sums_ref),
+        (lift_hbm, lift_ref),
+        (taps_hbm, taps_ref),
+        (point_hbm, point_ref),
+        (outw_hbm, outw_ref),
+    ]
+    loads = [pltpu.make_async_copy(a, b, sem.at[i]) for i, (a, b) in enumerate(pairs)]
+    pairs = [
+        (gv_in, gv_out),
+        (glift_ref, lift_out),
+        (gtaps_ref, taps_out),
+        (gpoint_ref, point_out),
+        (gout_ref, out_out),
+    ]
+    stores = [pltpu.make_async_copy(a, b, sem.at[5 + i]) for i, (a, b) in enumerate(pairs)]
+    for load in loads:
+        load.start()
+    stores[0].start()
+    for load in loads:
+        load.wait()
+    sums = sums_ref[...]
+    lift = lift_ref[...]
+    point = point_ref[0]
+    outw = outw_ref[...].astype(f32)
+    lift_wide, taps_wide = widened(lift, taps_ref[:, 0, :])
+    both = lift_wide * taps_wide
     gz_sum = jnp.concatenate([sums[:, :64], sums[:8, 64:]], axis=0)
     depth = dot(halved(gz_sum, 0), point)
     depth = depth[:24] + depth[24:]
@@ -733,17 +797,10 @@
         for r in range(2):
             total = total + sums[10 + r : 11 + r, 64 + s : 65 + s] * lift[r : r + 1]
         gout_ref[s : s + 1] = total
-    for copy in pending:
-        copy.wait_send()
-
-
-def hand_over(*refs):
-    sources, targets, sems = refs[:5], refs[5:10], refs[10]
-    copies = [pltpu.make_async_copy(sources[i], targets[i], sems.at[i]) for i in range(5)]
-    for copy in copies:
-        copy.start()
-    for copy in copies:
-        copy.wait()
+    for store in stores[1:]:
+        store.start()
+    for store in stores:
+        store.wait()
 
 
 def fused(velocity, cotangent, lift_weight, depth_kernels, point_weights, out_weight):
@@ -755,20 +812,21 @@
     wide = cols + 128
     tables = make_tables(groups_y, groups_x, rows, cols)
     bf16, f32 = jnp.bfloat16, jnp.float32
-    vmem = pl.BlockSpec(memory_space=pltpu.VMEM)
     dma = pltpu.SemaphoreType.DMA
-    results = pl.pallas_call(
+    hbm = pl.BlockSpec(memory_space=pltpu.HBM)
+    lift_t = lift_weight.T
+    taps_t = jnp.transpose(depth_kernels, (2, 0, 1))
+    grad_velocity, sums = pl.pallas_call(
         functools.partial(fused_kernel, groups_y, groups_x, rows, cols),
         out_shape=(
             jax.ShapeDtypeStruct((2, rows, cols), f32),
-            jax.ShapeDtypeStruct((2, channels), f32),
-            jax.ShapeDtypeStruct((9, 1, channels), f32),
-            jax.ShapeDtypeStruct((1, channels, channels), f32),
-            jax.ShapeDtypeStruct((2, channels), f32),
+            jax.ShapeDtypeStruct((16, 128), f32),
         ),
-        in_specs=[pl.BlockSpec(memory_space=pltpu.HBM)] * 10,
-        out_specs=(vmem,) * 5,
+        in_specs=[hbm] * 10,
+        out_specs=(hbm, hbm),
         scratch_shapes=[
+            pltpu.VMEM((2, rows, cols), f32),
+            pltpu.VMEM((16, 128), f32),
             pltpu.VMEM((2, rows, cols), f32),
             pltpu.VMEM((2, rows, cols), f32),
             pltpu.VMEM((2, channels), f32),
@@ -797,7 +855,7 @@
             pltpu.VMEM((wide // 128, 24 * (rows + 2), 128), f32),
             pltpu.VMEM((groups_y, 16, 128), f32),
             pltpu.VMEM((groups_x, 16, 128), f32),
-            dma((10,)),
+            dma((12,)),
             dma((groups_y,)),
             dma((groups_y,)),
             dma((groups_x,)),
@@ -821,20 +879,37 @@
     )(
         velocity,
         cotangent,
-        lift_weight.T,
-        jnp.transpose(depth_kernels, (2, 0, 1)),
+        lift_t,
+        taps_t,
         point_weights,
         out_weight,
         *[jnp.asarray(t) for t in tables],
     )
     results = pl.pallas_call(
-        hand_over,
-        out_shape=[jax.ShapeDtypeStruct(r.shape, r.dtype) for r in results],
-        in_specs=[pl.BlockSpec(memory_space=pltpu.HBM)] * 5,
-        out_specs=[pl.BlockSpec(memory_space=pltpu.HBM)] * 5,
-        scratch_shapes=[dma((5,))],
+        finish_kernel,
+        out_shape=(
+            jax.ShapeDtypeStruct((2, rows, cols), f32),
+            jax.ShapeDtypeStruct((2, channels), f32),
+            jax.ShapeDtypeStruct((9, 1, channels), f32),
+            jax.ShapeDtypeStruct((1, channels, channels), f32),
+            jax.ShapeDtypeStruct((2, channels), f32),
+        ),
+        in_specs=[hbm] * 6,
+        out_specs=(hbm,) * 5,
+        scratch_shapes=[
+            pltpu.VMEM((16, 128), f32),
+            pltpu.VMEM((2, channels), f32),
+            pltpu.VMEM((9, 1, channels), f32),
+            pltpu.VMEM((1, channels, channels), bf16),
+            pltpu.VMEM((2, channels), bf16),
+            pltpu.VMEM((2, channels), f32),
+            pltpu.VMEM((9, 1, channels), f32),
+            pltpu.VMEM((1, channels, channels), f32),
+            pltpu.VMEM((2, channels), f32),
+            dma((10,)),
+        ],
         compiler_params=pltpu.CompilerParams(vmem_limit_bytes=64 * 1024 * 1024),
-    )(*results)
+    )(grad_velocity, sums, lift_t, taps_t, point_weights, out_weight)
     grad_velocity, grad_lift, grad_taps, grad_point, grad_out = results
     return grad_velocity, grad_lift.T, jnp.transpose(grad_taps, (1, 2, 0)), grad_point, grad_out
 

time: 40.6 us -> 39.2 us (0.966)
  Pallas kernels: 39.8 us -> 38.3 us
    pallas_call x1, Pallas kernels: 4.33 us -> 3.19 us  [fused(): pl.pallas_call(finish_kernel, out_shape=(jax.ShapeDtypeStruct((2, rows, c...]
where the time goes in v3:
time: 39.2 us; the launch traced here: 39 us
  Pallas kernels  38.3 us (98%)
  between operations  0.64 us (2%)
    pallas_call x1, Pallas kernels, fused(): pl.pallas_call(functools.partial(fused_kernel, groups_y, groups_x, rows,...  35.1 us
    pallas_call x1, Pallas kernels, fused(): pl.pallas_call(finish_kernel, out_shape=(jax.ShapeDtypeStruct((2, rows, c...  3.19 us

profile of v3, /device:TPU:0, one launch (start us, length us, event | category | flops | bytes accessed | tf_op | source)
XLA Modules:
  0.0 39.0 jit_solution(14920098190100796945)
XLA Ops:
  0.6 35.1 %shard_map.137 = (f32[2,32,256]{2,1,0:T(8,128)}, f32[16,128]{1,0:T(8,128)}) custom-call(f32[2,32,256]{2,1,0:T(8,128)} %vel_hbm.1, f32[2,32,256]{2,1,0:T(8,128)} %cot_hbm.1, f32[2,64]{1,0:T(2,128)} %bitcast.6, f32[9,1,64]{2,1,0:T(1,128)} %bitcast.4, bf16[1,64,64]{2,1,0:T(8,128)(2,1)} %point_hbm.3, bf16[2,64]{1,0:T(2,128)(2,1)} %outw_hbm.3, ...), custom_call_target="tpu_custom_call" | custom-call | tf_op jit(solution)/shard_map/pallas_call | solution.py:819
  35.8 3.2 %shard_map.138 = (f32[2,32,256]{2,1,0:T(8,128)}, f32[2,64]{1,0:T(2,128)}, f32[9,1,64]{2,1,0:T(1,128)}, f32[1,64,64]{2,1,0:T(8,128)}, f32[2,64]{1,0:T(2,128)}) custom-call(f32[2,32,256]{2,1,0:T(8,128)} %get-tuple-element.12.gv_in, f32[16,128]{1,0:T(8,128)} %get-tuple-element.13.sums_hbm, f32[2,64]{1,0:T(2,128)} %bitcast.7, f32[9,1,64]{2,1,0:T(1,128)} %bitcast.5, ...), custom_call_target="tpu_custom_call" | custom-call | tf_op jit(solution)/shard_map/pallas_call | solution.py:888

commit v4 on v3

--- a/solution.py
+++ b/solution.py
@@ -600,7 +600,7 @@
     loads[3].wait()
     split = halved(jnp.concatenate([p0, p1], axis=1), 0)
     fields = dot(split, ix[0])
-    fields = (fields[:per] + fields[per:] + dot(split[:per], ix[1])).astype(bf16)
+    fields = fields[:per] + fields[per:] + dot(split[:per], ix[1])
     for dst in range(groups_x):
         send3[dst] = fields[:, dst * 128 : (dst + 1) * 128]
     pending += spread_x(lambda dst: send3.at[dst], recv3, s3, r3)
@@ -621,8 +621,7 @@
 
     for step in range(1, groups_x):
         arrived_x(recv3, s3, r3, step)
-    turned = jnp.transpose(recv3[...].reshape(cols, 128).astype(f32))
-    gath4[h] = turned[: 2 * band].astype(bf16)
+    gath4[h] = halved(jnp.transpose(recv3[...].reshape(cols, 128))[: 2 * band], 0)
     pending += spread_y(gath4, s4, r4)
 
     forward_rows(16, rows - 16)
@@ -634,7 +633,9 @@
         src = h if step == 0 else arrived_y(gath4, s4, r4, step)
         where = pl.ds(pl.multiple_of(src * cols, cols), cols)
         got = gath4[src]
-        field = field + dot(got, iy[0, where, :]) + dot(got, iy[1, where, :])
+        both_parts = dot(got, iy[0, where, :])
+        field = field + both_parts[: 2 * band] + both_parts[2 * band :]
+        field = field + dot(got[: 2 * band], iy[1, where, :])
     gp2[...] = jnp.zeros_like(gp2)
     for s in range(2):
         part = field[s * band : (s + 1) * band]
@@ -840,9 +841,9 @@
             pltpu.VMEM((groups_y, 4 * rows, cols), bf16),
             pltpu.VMEM((groups_x, per, 4 * rows), bf16),
             pltpu.VMEM((groups_x, per, 4 * rows), bf16),
-            pltpu.VMEM((groups_x, per, 128), bf16),
-            pltpu.VMEM((groups_x, per, 128), bf16),
-            pltpu.VMEM((groups_y, 2 * (rows + 8), cols), bf16),
+            pltpu.VMEM((groups_x, per, 128), f32),
+            pltpu.VMEM((groups_x, per, 128), f32),
+            pltpu.VMEM((groups_y, 4 * (rows + 8), cols), bf16),
             pltpu.VMEM((2, 2 * rows, 128), f32),
             pltpu.VMEM((2, 2 * rows, 128), f32),
             pltpu.VMEM((2, 8, wide), f32),

time: 39.2 us -> 41.9 us (1.069)
  Pallas kernels: 38.3 us -> 41 us
    pallas_call x1, Pallas kernels: 35.1 us -> 37.9 us  [fused(): pl.pallas_call(functools.partial(fused_kernel, groups_y, groups_x, rows,...]
where the time goes in v4:
time: 41.9 us; the launch traced here: 41.7 us
  Pallas kernels  41 us (98%)
  between operations  0.64 us (2%)
    pallas_call x1, Pallas kernels, fused(): pl.pallas_call(functools.partial(fused_kernel, groups_y, groups_x, rows,...  37.9 us
    pallas_call x1, Pallas kernels, fused(): pl.pallas_call(finish_kernel, out_shape=(jax.ShapeDtypeStruct((2, rows, c...  3.19 us

profile of v4, /device:TPU:0, one launch (start us, length us, event | category | flops | bytes accessed | tf_op | source)
XLA Modules:
  0.0 41.7 jit_solution(2191335301710883949)
XLA Ops:
  0.6 37.9 %shard_map.137 = (f32[2,32,256]{2,1,0:T(8,128)}, f32[16,128]{1,0:T(8,128)}) custom-call(f32[2,32,256]{2,1,0:T(8,128)} %vel_hbm.1, f32[2,32,256]{2,1,0:T(8,128)} %cot_hbm.1, f32[2,64]{1,0:T(2,128)} %bitcast.6, f32[9,1,64]{2,1,0:T(1,128)} %bitcast.4, bf16[1,64,64]{2,1,0:T(8,128)(2,1)} %point_hbm.3, bf16[2,64]{1,0:T(2,128)(2,1)} %outw_hbm.3, ...), custom_call_target="tpu_custom_call" | custom-call | tf_op jit(solution)/shard_map/pallas_call | solution.py:820
  38.5 3.2 %shard_map.138 = (f32[2,32,256]{2,1,0:T(8,128)}, f32[2,64]{1,0:T(2,128)}, f32[9,1,64]{2,1,0:T(1,128)}, f32[1,64,64]{2,1,0:T(8,128)}, f32[2,64]{1,0:T(2,128)}) custom-call(f32[2,32,256]{2,1,0:T(8,128)} %get-tuple-element.12.gv_in, f32[16,128]{1,0:T(8,128)} %get-tuple-element.13.sums_hbm, f32[2,64]{1,0:T(2,128)} %bitcast.7, f32[9,1,64]{2,1,0:T(1,128)} %bitcast.5, ...), custom_call_target="tpu_custom_call" | custom-call | tf_op jit(solution)/shard_map/pallas_call | solution.py:889
